TPU v7x, 128 devices: a whole 4x4x4 slice. The times are simulated.
128 devices in a mesh: slide: 8 (over x, core), tile: 16 (over y, z).
Axes of the slice: x: 4, y: 4, z: 4, core: 2. Of those that a mesh axis runs over, the one named last changes fastest.
Arguments:
- tiles: float32 [4096, 1536], P(('slide', 'tile')), may hold values from -6 to 6
- mlp_gain: float32 [1536], replicated, may hold values from 0.25 to 1.75
- mlp_bias: float32 [1536], replicated, may hold values from -0.5 to 0.5
- gate_weight: bfloat16 [1536, 4096], P(None, 'tile'), may hold values from -0.15625 to 0.15625
- up_weight: bfloat16 [1536, 4096], P(None, 'tile'), may hold values from -0.15625 to 0.15625
- down_weight: bfloat16 [4096, 1536], P('tile'), may hold values from -0.09375 to 0.09375
- layer_scale: float32 [1536], replicated, may hold values from 0.1 to 1
- final_gain: float32 [1536], replicated, may hold values from 0.25 to 1.75
- final_bias: float32 [1536], replicated, may hold values from -0.5 to 0.5
- patch_weight: bfloat16 [1536, 768], replicated, may hold values from -0.15625 to 0.15625
- patch_bias: float32 [768], replicated, may hold values from -0.5 to 0.5
- slide_gain: float32 [768], replicated, may hold values from 0.25 to 1.75
- slide_bias: float32 [768], replicated, may hold values from -0.5 to 0.5
- w_query: float32 [768, 768], replicated
- w_key: float32 [768, 768], replicated
- w_value: float32 [768, 768], replicated, may hold values from -0.21875 to 0.21875
- w_out: float32 [768, 768], replicated, may hold values from -0.21875 to 0.21875
- slide_lengths: int32 [16], replicated, may hold values from 1 to 512, as said below
- tile_slot: int32 [4096], P(('slide', 'tile')), may hold values from 0 to 8191, as said below
Outputs:
- slide_out: float32 [16, 512, 768], P('tile', 'slide')
Inputs may be any that keep to these rules, and one draw needn't show every extreme that they name: `slide_lengths`: tile counts of the slides: they sum to 4096, the largest is exactly 512, and every slide has at least one tile. tile_slot[t] = s * 512 + p puts tile t at position p of slide s; slide s uses exactly the positions 0 to slide_lengths[s] - 1, each once. The tiles of one device fall at most 1 at a time into one block of 64 consecutive positions of a slide that starts at a multiple of 64; every draw reaches 1 for every device in some block that is filled.
All inputs are finite; a program needn't handle non-finite values.
Results may differ from a plain program's by a relative error of at most 0.027.
Values may be sent and summed in bfloat16 or wider, within the bound.
A program may use at most 128 MiB of HBM per device.

v0:
```python
import jax
import jax.numpy as jnp
from jax import lax
from jax.experimental import pallas as pl
from jax.experimental.pallas import tpu as pltpu
from jax.sharding import PartitionSpec as P

D_TILE = 1536
D_SLIDE = 768
HEADS = 16
HEAD_DIM = 48
TILE_DEV = 32
SEQ_DEV = 64
SEQ = 512
GROUP = 256
MESH = pl.DeviceIdType.MESH
F32 = jnp.float32
BF16 = jnp.bfloat16
epsilon = 1e-06
masked_score = -1e30


def layer_norm(values, scale_vec, shift_vec):
    average = jnp.mean(values, axis=-1, keepdims=True)
    centred = values - average
    variance = jnp.mean(centred * centred, axis=-1, keepdims=True)
    return centred * lax.rsqrt(variance + epsilon) * scale_vec + shift_vec


def iota(shape, dim):
    return lax.broadcasted_iota(jnp.int32, shape, dim)


def offset_of(i):
    return i + (i // 2) * (1 - 2 * (i % 2))


def kernel(
    tiles_h, mlp_gain_h, mlp_bias_h, gate_h, up_h, down_h, layer_scale_h, final_gain_h, final_bias_h,
    patch_h, patch_bias_h, slide_gain_h, slide_bias_h, wq_h, wk_h, wv_h, wo_h, lengths, slot_h,
    out,
    tiles, mlp_gain, mlp_bias, gate, up, down, layer_scale, final_gain, final_bias,
    patch, patch_bias, slide_gain, slide_bias, wq, wk, wv, wo, slot,
    rows, part, got1, fold, got2, wkv16, wq16, wo16,
    pos_out, pos_in, pos_all, send_slots, got_slots, slots, one_hot, canvas, normed_all, kv, mult, att,
    load_sem, ag1_s, ag2_s, ag_r, rs1_s, rs1_r, rs2_s, rs2_r,
    pos_s, pos_r, pa_s, pa_r, sl_s, sl_r, dg_s, dg_r,
):
    s = lax.axis_index("slide")
    t = lax.axis_index("tile")
    x, c = s // 2, s % 2
    y, z = t // 4, t % 4

    def first(k):
        return (s, ((y + c * k) % 4) * 4 + (z + (1 - c) * k) % 4)

    def second(k):
        return (s, ((y + (1 - c) * k) % 4) * 4 + (z + c * k) % 4)

    def on_tile(k):
        return (s, (t + k) % 16)

    def on_slide(dx, dc):
        return (((x + dx) % 4) * 2 + (c + dc) % 2, t)

    def remote(src, dst, send_sem, recv_sem, device):
        return pltpu.make_async_remote_copy(
            src_ref=src, dst_ref=dst, send_sem=send_sem, recv_sem=recv_sem,
            device_id=device, device_id_type=MESH,
        )

    pairs = (
        (tiles_h, tiles), (mlp_gain_h, mlp_gain), (mlp_bias_h, mlp_bias), (slot_h, slot),
        (gate_h, gate), (up_h, up), (down_h, down), (layer_scale_h, layer_scale),
        (final_gain_h, final_gain), (final_bias_h, final_bias), (patch_h, patch), (patch_bias_h, patch_bias),
        (wk_h, wk), (wv_h, wv), (wq_h, wq), (wo_h, wo), (slide_gain_h, slide_gain), (slide_bias_h, slide_bias),
    )
    loads = [pltpu.make_async_copy(a, b, load_sem.at[i]) for i, (a, b) in enumerate(pairs)]
    for load in loads:
        load.start()

    barrier = pltpu.get_barrier_semaphore()

    def greet(k, carry):
        pl.semaphore_signal(barrier, inc=1, device_id=on_tile(k), device_id_type=MESH)
        return carry

    lax.fori_loop(1, 16, greet, 0)

    def greet_slide(k, carry):
        pl.semaphore_signal(barrier, inc=1, device_id=on_slide(k // 2, k % 2), device_id_type=MESH)
        return carry

    lax.fori_loop(1, 8, greet_slide, 0)

    for i in range(3):
        loads[i].wait()
    rows[0] = layer_norm(tiles[...], mlp_gain[...], mlp_bias[...]).astype(BF16)

    pl.semaphore_wait(barrier, 22)

    def ag1(j):
        return remote(rows.at[0], rows.at[j], ag1_s.at[j], ag_r.at[j], first(offset_of(j)))

    for j in range(1, 4):
        ag1(j).start()

    def ag2(i, j):
        return remote(
            rows.at[j], rows.at[i * 4 + j], ag2_s.at[i * 4 + j], ag_r.at[i * 4 + j], second(offset_of(i))
        )

    for i in range(1, 4):
        ag2(i, 0).start()

    loads[3].wait()
    spot = slot[...]
    row_id = iota((128, TILE_DEV), 0)
    match = (spot // 512 == row_id // 8) & ((spot // 64) % 8 == row_id % 8)
    place = jnp.sum(jnp.where(match, (spot % 512 + 1).astype(F32), 0.0), axis=1, keepdims=True)
    pos_out[...] = jnp.broadcast_to(place, (128, 128)).reshape(16, 8, 128)
    pos_in[0] = pos_out[t]

    def pos_copy(k):
        return remote(pos_out.at[(t + k) % 16], pos_in.at[k], pos_s.at[k], pos_r.at[k], on_tile(k))

    def pos_start(k, carry):
        pos_copy(k).start()
        return carry

    lax.fori_loop(1, 16, pos_start, 0)

    for j in range(1, 4):
        ag1(j).wait_recv()
        for i in range(1, 4):
            ag2(i, j).start()

    def pos_wait(k, carry):
        pos_copy(k).wait_recv()
        return carry

    lax.fori_loop(1, 16, pos_wait, 0)
    turned = jnp.transpose(pos_in[...].reshape(128, 128))
    pos_all[0] = turned[0:8]

    def pa_copy(k):
        return remote(pos_all.at[0], pos_all.at[k], pa_s.at[k], pa_r.at[k], on_slide(k // 2, k % 2))

    def pa_start(k, carry):
        pa_copy(k).start()
        return carry

    lax.fori_loop(1, 8, pa_start, 0)

    for i in range(4, 7):
        loads[i].wait()

    def rs1(i):
        return remote(
            part.at[pl.ds(4 * i, 4)], got1.at[i - 1], rs1_s.at[i], rs1_r.at[i], second(4 - offset_of(i))
        )

    def batch(i, carry):
        @pl.when(i > 0)
        def _():
            for j in range(4):
                ag2(i, j).wait_recv()

        block = rows[pl.ds(4 * i, 4)].reshape(128, D_TILE)
        gate_out = jnp.dot(block, gate[...], preferred_element_type=F32)
        up_out = jnp.dot(block, up[...], preferred_element_type=F32)
        hidden = (gate_out / (1.0 + jnp.exp(-gate_out)) * up_out).astype(BF16)
        part[pl.ds(4 * i, 4)] = (
            jnp.dot(hidden, down[...], preferred_element_type=F32).astype(BF16).reshape(4, TILE_DEV, D_TILE)
        )

        @pl.when(i > 0)
        def _():
            rs1(i).start()

        return carry

    lax.fori_loop(0, 4, batch, 0)

    for i in range(12, 16):
        loads[i].wait()

    def convert(k, carry):
        at = pl.ds(pl.multiple_of(k * 128, 128), 128)
        wkv16[at, 0:D_SLIDE] = wk[at, :].astype(BF16)
        wkv16[at, D_SLIDE : 2 * D_SLIDE] = wv[at, :].astype(BF16)
        wq16[at, :] = wq[at, :].astype(BF16)
        wo16[at, :] = wo[at, :].astype(BF16)
        return carry

    lax.fori_loop(0, 6, convert, 0)

    def pa_wait(k, carry):
        pa_copy(k).wait_recv()
        return carry

    lax.fori_loop(1, 8, pa_wait, 0)
    position = (iota((SEQ, 128), 0) + 1).astype(F32)
    for k in range(8):
        one_hot[:, k * 128 : (k + 1) * 128] = jnp.where(position == pos_all[k][0:1], 1.0, 0.0).astype(BF16)

    length = lengths[t]
    row = iota((256, SEQ), 0)
    key = iota((256, SEQ), 1)
    head, query = row // 64, row % 64
    weight = (
        1.0
        + jnp.where((query % 2 == head % 2) & (key % 2 == head % 2), 1.0, 0.0)
        + jnp.where((query % 4 == head) & (key % 4 == head), 1.0, 0.0)
    )
    mult[...] = jnp.where(key < length, weight, 0.0)

    for i in range(1, 4):
        rs1(i).wait_recv()

    def rs2(j):
        return remote(fold.at[j - 1], got2.at[j - 1], rs2_s.at[j], rs2_r.at[j], first(4 - offset_of(j)))

    def line_sum(j):
        return (
            part[j].astype(F32) + got1[0, j].astype(F32) + got1[1, j].astype(F32) + got1[2, j].astype(F32)
        )

    for j in range(1, 4):
        fold[j - 1] = line_sum(j).astype(BF16)
        rs2(j).start()
    mixed = line_sum(0)
    for i in range(7, 12):
        loads[i].wait()
    for j in range(1, 4):
        rs2(j).wait_recv()
    mixed = mixed + got2[0].astype(F32) + got2[1].astype(F32) + got2[2].astype(F32)
    final = layer_norm(tiles[...] + layer_scale[...] * mixed, final_gain[...], final_bias[...]).astype(BF16)
    embed = (jnp.dot(final, patch[...], preferred_element_type=F32) + patch_bias[...]).astype(BF16)

    slot_id = iota((256, TILE_DEV), 0)
    hit = (spot // 512 == slot_id // 16) & ((spot // 64) % 8 == slot_id % 8)
    left = jnp.where(hit & (slot_id % 16 < 8), 1.0, 0.0).astype(BF16)
    right = jnp.where(hit & (slot_id % 16 >= 8), 1.0, 0.0).astype(BF16)
    send_slots[...] = (
        (
            jnp.dot(left, embed[:, 0:384], preferred_element_type=F32)
            + jnp.dot(right, embed[:, 384:768], preferred_element_type=F32)
        )
        .astype(BF16)
        .reshape(16, 16, 384)
    )

    def slot_copy(k):
        return remote(send_slots.at[(t + k) % 16], got_slots.at[k], sl_s.at[k], sl_r.at[k], on_tile(k))

    def slot_start(k, carry):
        slot_copy(k).start()
        return carry

    lax.fori_loop(1, 16, slot_start, 0)
    got_slots[0] = send_slots[t]

    def slot_wait(k, carry):
        slot_copy(k).wait_recv()
        return carry

    lax.fori_loop(1, 16, slot_wait, 0)
    wide = got_slots[...].astype(F32)
    slots[0, :, 0:384] = wide[:, 0:8, :].reshape(128, 384).astype(BF16)
    slots[0, :, 384:768] = wide[:, 8:16, :].reshape(128, 384).astype(BF16)

    def far(i):
        k = 2 * offset_of(i)
        return remote(slots.at[0], slots.at[k], dg_s.at[k], dg_r.at[k], on_slide(offset_of(i), 0))

    def near(i):
        k = 2 * offset_of(i)
        return remote(slots.at[k], slots.at[k + 1], dg_s.at[k + 1], dg_r.at[k + 1], on_slide(0, 1))

    for i in range(1, 4):
        far(i).start()
    near(0).start()

    def place_pair(i):
        k = 2 * offset_of(i)
        return jnp.dot(
            one_hot[:, k * 128 : (k + 2) * 128], slots[k : k + 2].reshape(256, D_SLIDE), preferred_element_type=F32
        )

    near(0).wait_recv()
    canvas[...] = place_pair(0)
    for i in range(1, 4):
        far(i).wait_recv()
        near(i).start()
    for i in range(1, 4):
        near(i).wait_recv()
        canvas[...] += place_pair(i)
    for i in range(16, 18):
        loads[i].wait()
    normed_all[...] = layer_norm(canvas[...], slide_gain[...], slide_bias[...]).astype(BF16)
    mine = pl.ds(pl.multiple_of(s * SEQ_DEV, SEQ_DEV), SEQ_DEV)
    kv[...] = jnp.dot(normed_all[...], wkv16[...], preferred_element_type=F32).astype(BF16)
    queries = jnp.dot(normed_all[mine, :], wq16[...], preferred_element_type=F32) * HEAD_DIM ** (-0.5)

    head_row = iota((256, 256), 0) // 64
    lane = iota((256, 256), 1)
    att[...] = jnp.zeros_like(att)
    for w, start in enumerate((0, 128, 384, 512)):
        low = (4 * w + head_row) * HEAD_DIM - start
        own = (lane >= low) & (lane < low + HEAD_DIM)
        window = queries[:, start : start + 256]
        stacked = jnp.where(own, jnp.concatenate([window] * 4, axis=0), 0.0).astype(BF16)
        scores = lax.dot_general(
            stacked, kv[:, start : start + 256], (((1,), (1,)), ((), ())), preferred_element_type=F32
        )
        counted = mult[...]
        scores = jnp.where(counted > 0.0, scores, masked_score)
        weights = jnp.exp(scores - jnp.max(scores, axis=1, keepdims=True)) * counted
        total = jnp.sum(weights, axis=1, keepdims=True)
        mixed_rows = jnp.dot(
            weights.astype(BF16), kv[:, D_SLIDE + start : D_SLIDE + start + 256], preferred_element_type=F32
        )
        mixed_rows = jnp.where(own, mixed_rows / total, 0.0)
        att[:, start : start + 256] += (
            mixed_rows[0:64] + mixed_rows[64:128] + mixed_rows[128:192] + mixed_rows[192:256]
        )
    result = canvas[mine, :] + jnp.dot(att[...].astype(BF16), wo16[...], preferred_element_type=F32)
    here = iota((SEQ_DEV, D_SLIDE), 0) + s * SEQ_DEV
    out[0] = jnp.where(here < length, result, 0.0)

    for j in range(1, 4):
        ag1(j).wait_send()
        rs1(j).wait_send()
        rs2(j).wait_send()
        far(j).wait_send()
        for i in range(0, 4):
            ag2(j, i).wait_send()
    for i in range(4):
        near(i).wait_send()

    def sent(k, carry):
        pos_copy(k).wait_send()
        slot_copy(k).wait_send()
        return carry

    lax.fori_loop(1, 16, sent, 0)

    def sent_pa(k, carry):
        pa_copy(k).wait_send()
        return carry

    lax.fori_loop(1, 8, sent_pa, 0)


def per_device(
    tiles, mlp_gain, mlp_bias, gate_weight, up_weight, down_weight, layer_scale, final_gain, final_bias,
    patch_weight, patch_bias, slide_gain, slide_bias, w_query, w_key, w_value, w_out, slide_lengths, tile_slot,
):
    wide = lambda v: v.reshape(1, -1)
    hbm = pl.BlockSpec(memory_space=pl.ANY)
    dma = pltpu.SemaphoreType.DMA
    vm = pltpu.VMEM
    return pl.pallas_call(
        kernel,
        out_shape=jax.ShapeDtypeStruct((1, SEQ_DEV, D_SLIDE), F32),
        in_specs=[hbm] * 17 + [pl.BlockSpec(memory_space=pltpu.SMEM)] + [hbm],
        out_specs=pl.BlockSpec(memory_space=pltpu.VMEM),
        scratch_shapes=[
            vm((TILE_DEV, D_TILE), F32), vm((1, D_TILE), F32), vm((1, D_TILE), F32),
            vm((D_TILE, GROUP), BF16), vm((D_TILE, GROUP), BF16), vm((GROUP, D_TILE), BF16),
            vm((1, D_TILE), F32), vm((1, D_TILE), F32), vm((1, D_TILE), F32),
            vm((D_TILE, D_SLIDE), BF16), vm((1, D_SLIDE), F32), vm((1, D_SLIDE), F32), vm((1, D_SLIDE), F32),
            vm((D_SLIDE, D_SLIDE), F32), vm((D_SLIDE, D_SLIDE), F32),
            vm((D_SLIDE, D_SLIDE), F32), vm((D_SLIDE, D_SLIDE), F32),
            vm((1, TILE_DEV), jnp.int32),
            vm((16, TILE_DEV, D_TILE), BF16), vm((16, TILE_DEV, D_TILE), BF16),
            vm((3, 4, TILE_DEV, D_TILE), BF16), vm((3, TILE_DEV, D_TILE), BF16), vm((3, TILE_DEV, D_TILE), BF16),
            vm((D_SLIDE, 2 * D_SLIDE), BF16), vm((D_SLIDE, D_SLIDE), BF16), vm((D_SLIDE, D_SLIDE), BF16),
            vm((16, 8, 128), F32), vm((16, 8, 128), F32), vm((8, 8, 128), F32),
            vm((16, 16, 384), BF16), vm((16, 16, 384), BF16), vm((8, 128, D_SLIDE), BF16),
            vm((SEQ, 1024), BF16), vm((SEQ, D_SLIDE), F32), vm((SEQ, D_SLIDE), BF16),
            vm((SEQ, 2 * D_SLIDE), BF16), vm((256, SEQ), F32), vm((SEQ_DEV, D_SLIDE), F32),
            dma((18,)), dma((4,)), dma((16,)), dma((16,)), dma((4,)), dma((4,)), dma((4,)), dma((4,)),
            dma((16,)), dma((16,)), dma((8,)), dma((8,)), dma((16,)), dma((16,)), dma((8,)), dma((8,)),
        ],
        compiler_params=pltpu.CompilerParams(
            collective_id=0, has_side_effects=True, vmem_limit_bytes=56 * 2**20
        ),
        name="slide_kernel",
    )(
        tiles, wide(mlp_gain), wide(mlp_bias), gate_weight, up_weight, down_weight, wide(layer_scale),
        wide(final_gain), wide(final_bias), patch_weight, wide(patch_bias), wide(slide_gain), wide(slide_bias),
        w_query, w_key, w_value, w_out, slide_lengths, wide(tile_slot),
    )


def solution(mesh):
    both = P(("slide", "tile"))
    placed = (
        P(("slide", "tile"), None), P(), P(), P(None, "tile"), P(None, "tile"), P("tile", None),
        P(), P(), P(), P(), P(), P(), P(), P(), P(), P(), P(), P(), both,
    )
    return jax.shard_map(
        per_device, mesh=mesh, in_specs=placed, out_specs=P("tile", "slide", None), check_vma=False
    )
```

profile of v0, /device:TPU:1, one launch (start us, length us, event | category | flops | bytes accessed | tf_op | source)
XLA Modules:
  0.0 77.2 jit_solution(1985193584192903603)
XLA Ops:
  0.0 1.3 %reshape.32.patch_bias_h = f32[1,768]{1,0:T(1,128)} reshape(f32[768]{0:T(1024)} %param.29) | data formatting | bytes 6144 | tf_op jit(solution)/shard_map/reshape | solution.py:360
  1.3 1.3 %reshape.33.slide_gain_h = f32[1,768]{1,0:T(1,128)} reshape(f32[768]{0:T(1024)} %param.30) | data formatting | bytes 6144 | tf_op jit(solution)/shard_map/reshape | solution.py:360
  2.5 1.3 %reshape.34.slide_bias_h = f32[1,768]{1,0:T(1,128)} reshape(f32[768]{0:T(1024)} %param.31) | data formatting | bytes 6144 | tf_op jit(solution)/shard_map/reshape | solution.py:360
  3.8 1.3 %reshape.27.mlp_gain_h = f32[1,1536]{1,0:T(1,128)} reshape(f32[1536]{0:T(1024)} %param.20) | data formatting | bytes 12288 | tf_op jit(solution)/shard_map/reshape | solution.py:360
  5.1 1.3 %reshape.28.mlp_bias_h = f32[1,1536]{1,0:T(1,128)} reshape(f32[1536]{0:T(1024)} %param.21) | data formatting | bytes 12288 | tf_op jit(solution)/shard_map/reshape | solution.py:360
  6.4 1.3 %reshape.29.layer_scale_h = f32[1,1536]{1,0:T(1,128)} reshape(f32[1536]{0:T(1024)} %param.25) | data formatting | bytes 12288 | tf_op jit(solution)/shard_map/reshape | solution.py:360
  7.7 1.3 %reshape.30.final_gain_h = f32[1,1536]{1,0:T(1,128)} reshape(f32[1536]{0:T(1024)} %param.26) | data formatting | bytes 12288 | tf_op jit(solution)/shard_map/reshape | solution.py:360
  9.0 1.3 %reshape.31.final_bias_h = f32[1,1536]{1,0:T(1,128)} reshape(f32[1536]{0:T(1024)} %param.27) | data formatting | bytes 12288 | tf_op jit(solution)/shard_map/reshape | solution.py:360
  10.3 65.3 %slide_kernel.1 = f32[1,64,768]{2,1,0:T(8,128)} custom-call(f32[32,1536]{1,0:T(8,128)} %tiles_h.1, f32[1,1536]{1,0:T(1,128)} %reshape.27.mlp_gain_h, f32[1,1536]{1,0:T(1,128)} %reshape.28.mlp_bias_h, bf16[1536,256]{1,0:T(8,128)(2,1)} %gate_h.1, bf16[1536,256]{1,0:T(8,128)(2,1)} %up_h.1, bf16[256,1536]{1,0:T(8,128)(2,1)} %down_h.1, ...), custom_call_target="tpu_custom_call" | custom-call | tf_op jit(solution)/shard_map/slide_kernel/pallas_call | solution.py:364
  75.6 1.6 %copy.21 = f32[1,64,768]{2,1,0:T(8,128)} copy(f32[1,64,768]{2,1,0:T(8,128)} %slide_kernel.1) | data formatting | bytes 393216
where the time goes:
time: 78.6 us; the launch traced here: 77.2 us
  Pallas kernels  65.3 us (83%)
  local copies, waits for them, and re-layouts  11.9 us (15%)
    pallas_call x1, Pallas kernels, per_device(): pl.pallas_call(kernel, out_shape=jax.ShapeDtypeStruct((1, SEQ_DEV, D_SLID...  65.3 us
    reshape x8, local copies, waits for them, and re-layouts, per_device(): wide = lambda v: v.reshape(1, -1)  10.3 us
    unnamed x1, local copies, waits for them, and re-layouts  1.62 us

commit v1 on v0

--- a/solution.py
+++ b/solution.py
@@ -69,51 +69,89 @@
             device_id=device, device_id_type=MESH,
         )
 
+    pending = []
+
+    def sent(copy, first_k, last_k):
+        def one(k, carry):
+            copy(k).wait_send()
+            return carry
+
+        pending.append(lambda: lax.fori_loop(first_k, last_k, one, 0))
+
+    barrier = pltpu.get_barrier_semaphore()
+
+    def greet(device):
+        pl.semaphore_signal(barrier, inc=1, device_id=device, device_id_type=MESH)
+
+    for k in range(1, 4):
+        greet(first(k))
+        greet(second(k))
+    for k in range(1, 8):
+        greet(on_slide(k // 2, k % 2))
+
     pairs = (
-        (tiles_h, tiles), (mlp_gain_h, mlp_gain), (mlp_bias_h, mlp_bias), (slot_h, slot),
-        (gate_h, gate), (up_h, up), (down_h, down), (layer_scale_h, layer_scale),
+        (tiles_h, tiles), (mlp_gain_h, mlp_gain), (mlp_bias_h, mlp_bias),
+        (gate_h, gate), (up_h, up), (down_h, down), (slot_h, slot), (layer_scale_h, layer_scale),
         (final_gain_h, final_gain), (final_bias_h, final_bias), (patch_h, patch), (patch_bias_h, patch_bias),
         (wk_h, wk), (wv_h, wv), (wq_h, wq), (wo_h, wo), (slide_gain_h, slide_gain), (slide_bias_h, slide_bias),
     )
     loads = [pltpu.make_async_copy(a, b, load_sem.at[i]) for i, (a, b) in enumerate(pairs)]
     for load in loads:
         load.start()
-
-    barrier = pltpu.get_barrier_semaphore()
-
-    def greet(k, carry):
-        pl.semaphore_signal(barrier, inc=1, device_id=on_tile(k), device_id_type=MESH)
-        return carry
-
-    lax.fori_loop(1, 16, greet, 0)
-
-    def greet_slide(k, carry):
-        pl.semaphore_signal(barrier, inc=1, device_id=on_slide(k // 2, k % 2), device_id_type=MESH)
-        return carry
-
-    lax.fori_loop(1, 8, greet_slide, 0)
-
     for i in range(3):
         loads[i].wait()
     rows[0] = layer_norm(tiles[...], mlp_gain[...], mlp_bias[...]).astype(BF16)
 
-    pl.semaphore_wait(barrier, 22)
+    pl.semaphore_wait(barrier, 13)
 
     def ag1(j):
-        return remote(rows.at[0], rows.at[j], ag1_s.at[j], ag_r.at[j], first(offset_of(j)))
+        return remote(rows.at[0], rows.at[4 * j], ag1_s.at[j], ag_r.at[4 * j], first(offset_of(j)))
 
     for j in range(1, 4):
         ag1(j).start()
+        pending.append(ag1(j).wait_send)
 
     def ag2(i, j):
         return remote(
-            rows.at[j], rows.at[i * 4 + j], ag2_s.at[i * 4 + j], ag_r.at[i * 4 + j], second(offset_of(i))
+            rows.at[4 * j], rows.at[4 * j + i], ag2_s.at[4 * j + i], ag_r.at[4 * j + i], second(offset_of(i))
         )
 
     for i in range(1, 4):
         ag2(i, 0).start()
-
-    loads[3].wait()
+        pending.append(ag2(i, 0).wait_send)
+    for j in range(1, 4):
+        ag1(j).wait_recv()
+        for i in range(1, 4):
+            ag2(i, j).start()
+            pending.append(ag2(i, j).wait_send)
+    for i in range(3, 6):
+        loads[i].wait()
+
+    def rs1(i, j):
+        return remote(
+            part.at[4 * j + i], got1.at[j, i - 1], rs1_s.at[4 * j + i], rs1_r.at[4 * j + i], second(4 - offset_of(i))
+        )
+
+    def batch(j, carry):
+        for i in range(1, 4):
+            ag2(i, j).wait_recv()
+        block = rows[pl.ds(4 * j, 4)].reshape(128, D_TILE)
+        gate_out = jnp.dot(block, gate[...], preferred_element_type=F32)
+        up_out = jnp.dot(block, up[...], preferred_element_type=F32)
+        hidden = (gate_out / (1.0 + jnp.exp(-gate_out)) * up_out).astype(BF16)
+        part[pl.ds(4 * j, 4)] = (
+            jnp.dot(hidden, down[...], preferred_element_type=F32).astype(BF16).reshape(4, TILE_DEV, D_TILE)
+        )
+        for i in range(1, 4):
+            rs1(i, j).start()
+        return carry
+
+    lax.fori_loop(0, 4, batch, 0)
+    for j in range(4):
+        for i in range(1, 4):
+            pending.append(rs1(i, j).wait_send)
+
+    loads[6].wait()
     spot = slot[...]
     row_id = iota((128, TILE_DEV), 0)
     match = (spot // 512 == row_id // 8) & ((spot // 64) % 8 == row_id % 8)
@@ -129,58 +167,7 @@
         return carry
 
     lax.fori_loop(1, 16, pos_start, 0)
-
-    for j in range(1, 4):
-        ag1(j).wait_recv()
-        for i in range(1, 4):
-            ag2(i, j).start()
-
-    def pos_wait(k, carry):
-        pos_copy(k).wait_recv()
-        return carry
-
-    lax.fori_loop(1, 16, pos_wait, 0)
-    turned = jnp.transpose(pos_in[...].reshape(128, 128))
-    pos_all[0] = turned[0:8]
-
-    def pa_copy(k):
-        return remote(pos_all.at[0], pos_all.at[k], pa_s.at[k], pa_r.at[k], on_slide(k // 2, k % 2))
-
-    def pa_start(k, carry):
-        pa_copy(k).start()
-        return carry
-
-    lax.fori_loop(1, 8, pa_start, 0)
-
-    for i in range(4, 7):
-        loads[i].wait()
-
-    def rs1(i):
-        return remote(
-            part.at[pl.ds(4 * i, 4)], got1.at[i - 1], rs1_s.at[i], rs1_r.at[i], second(4 - offset_of(i))
-        )
-
-    def batch(i, carry):
-        @pl.when(i > 0)
-        def _():
-            for j in range(4):
-                ag2(i, j).wait_recv()
-
-        block = rows[pl.ds(4 * i, 4)].reshape(128, D_TILE)
-        gate_out = jnp.dot(block, gate[...], preferred_element_type=F32)
-        up_out = jnp.dot(block, up[...], preferred_element_type=F32)
-        hidden = (gate_out / (1.0 + jnp.exp(-gate_out)) * up_out).astype(BF16)
-        part[pl.ds(4 * i, 4)] = (
-            jnp.dot(hidden, down[...], preferred_element_type=F32).astype(BF16).reshape(4, TILE_DEV, D_TILE)
-        )
-
-        @pl.when(i > 0)
-        def _():
-            rs1(i).start()
-
-        return carry
-
-    lax.fori_loop(0, 4, batch, 0)
+    sent(pos_copy, 1, 16)
 
     for i in range(12, 16):
         loads[i].wait()
@@ -194,15 +181,6 @@
         return carry
 
     lax.fori_loop(0, 6, convert, 0)
-
-    def pa_wait(k, carry):
-        pa_copy(k).wait_recv()
-        return carry
-
-    lax.fori_loop(1, 8, pa_wait, 0)
-    position = (iota((SEQ, 128), 0) + 1).astype(F32)
-    for k in range(8):
-        one_hot[:, k * 128 : (k + 1) * 128] = jnp.where(position == pos_all[k][0:1], 1.0, 0.0).astype(BF16)
 
     length = lengths[t]
     row = iota((256, SEQ), 0)
@@ -215,21 +193,40 @@
     )
     mult[...] = jnp.where(key < length, weight, 0.0)
 
-    for i in range(1, 4):
-        rs1(i).wait_recv()
-
     def rs2(j):
         return remote(fold.at[j - 1], got2.at[j - 1], rs2_s.at[j], rs2_r.at[j], first(4 - offset_of(j)))
 
     def line_sum(j):
+        for i in range(1, 4):
+            rs1(i, j).wait_recv()
         return (
-            part[j].astype(F32) + got1[0, j].astype(F32) + got1[1, j].astype(F32) + got1[2, j].astype(F32)
+            part[4 * j].astype(F32) + got1[j, 0].astype(F32) + got1[j, 1].astype(F32) + got1[j, 2].astype(F32)
         )
 
     for j in range(1, 4):
         fold[j - 1] = line_sum(j).astype(BF16)
         rs2(j).start()
+        pending.append(rs2(j).wait_send)
     mixed = line_sum(0)
+
+    def pos_wait(k, carry):
+        pos_copy(k).wait_recv()
+        return carry
+
+    lax.fori_loop(1, 16, pos_wait, 0)
+    turned = jnp.transpose(pos_in[...].reshape(128, 128))
+    pos_all[0] = turned[0:8]
+
+    def pa_copy(k):
+        return remote(pos_all.at[0], pos_all.at[k], pa_s.at[k], pa_r.at[k], on_slide(k // 2, k % 2))
+
+    def pa_start(k, carry):
+        pa_copy(k).start()
+        return carry
+
+    lax.fori_loop(1, 8, pa_start, 0)
+    sent(pa_copy, 1, 8)
+
     for i in range(7, 12):
         loads[i].wait()
     for j in range(1, 4):
@@ -259,7 +256,17 @@
         return carry
 
     lax.fori_loop(1, 16, slot_start, 0)
+    sent(slot_copy, 1, 16)
     got_slots[0] = send_slots[t]
+
+    def pa_wait(k, carry):
+        pa_copy(k).wait_recv()
+        return carry
+
+    lax.fori_loop(1, 8, pa_wait, 0)
+    position = (iota((SEQ, 128), 0) + 1).astype(F32)
+    for k in range(8):
+        one_hot[:, k * 128 : (k + 1) * 128] = jnp.where(position == pos_all[k][0:1], 1.0, 0.0).astype(BF16)
 
     def slot_wait(k, carry):
         slot_copy(k).wait_recv()
@@ -280,7 +287,9 @@
 
     for i in range(1, 4):
         far(i).start()
+        pending.append(far(i).wait_send)
     near(0).start()
+    pending.append(near(0).wait_send)
 
     def place_pair(i):
         k = 2 * offset_of(i)
@@ -293,6 +302,7 @@
     for i in range(1, 4):
         far(i).wait_recv()
         near(i).start()
+        pending.append(near(i).wait_send)
     for i in range(1, 4):
         near(i).wait_recv()
         canvas[...] += place_pair(i)
@@ -329,35 +339,14 @@
     here = iota((SEQ_DEV, D_SLIDE), 0) + s * SEQ_DEV
     out[0] = jnp.where(here < length, result, 0.0)
 
-    for j in range(1, 4):
-        ag1(j).wait_send()
-        rs1(j).wait_send()
-        rs2(j).wait_send()
-        far(j).wait_send()
-        for i in range(0, 4):
-            ag2(j, i).wait_send()
-    for i in range(4):
-        near(i).wait_send()
-
-    def sent(k, carry):
-        pos_copy(k).wait_send()
-        slot_copy(k).wait_send()
-        return carry
-
-    lax.fori_loop(1, 16, sent, 0)
-
-    def sent_pa(k, carry):
-        pa_copy(k).wait_send()
-        return carry
-
-    lax.fori_loop(1, 8, sent_pa, 0)
+    for wait in pending:
+        wait()
 
 
 def per_device(
     tiles, mlp_gain, mlp_bias, gate_weight, up_weight, down_weight, layer_scale, final_gain, final_bias,
     patch_weight, patch_bias, slide_gain, slide_bias, w_query, w_key, w_value, w_out, slide_lengths, tile_slot,
 ):
-    wide = lambda v: v.reshape(1, -1)
     hbm = pl.BlockSpec(memory_space=pl.ANY)
     dma = pltpu.SemaphoreType.DMA
     vm = pltpu.VMEM
@@ -367,21 +356,21 @@
         in_specs=[hbm] * 17 + [pl.BlockSpec(memory_space=pltpu.SMEM)] + [hbm],
         out_specs=pl.BlockSpec(memory_space=pltpu.VMEM),
         scratch_shapes=[
-            vm((TILE_DEV, D_TILE), F32), vm((1, D_TILE), F32), vm((1, D_TILE), F32),
+            vm((TILE_DEV, D_TILE), F32), vm((D_TILE,), F32), vm((D_TILE,), F32),
             vm((D_TILE, GROUP), BF16), vm((D_TILE, GROUP), BF16), vm((GROUP, D_TILE), BF16),
-            vm((1, D_TILE), F32), vm((1, D_TILE), F32), vm((1, D_TILE), F32),
-            vm((D_TILE, D_SLIDE), BF16), vm((1, D_SLIDE), F32), vm((1, D_SLIDE), F32), vm((1, D_SLIDE), F32),
+            vm((D_TILE,), F32), vm((D_TILE,), F32), vm((D_TILE,), F32),
+            vm((D_TILE, D_SLIDE), BF16), vm((D_SLIDE,), F32), vm((D_SLIDE,), F32), vm((D_SLIDE,), F32),
             vm((D_SLIDE, D_SLIDE), F32), vm((D_SLIDE, D_SLIDE), F32),
             vm((D_SLIDE, D_SLIDE), F32), vm((D_SLIDE, D_SLIDE), F32),
             vm((1, TILE_DEV), jnp.int32),
             vm((16, TILE_DEV, D_TILE), BF16), vm((16, TILE_DEV, D_TILE), BF16),
-            vm((3, 4, TILE_DEV, D_TILE), BF16), vm((3, TILE_DEV, D_TILE), BF16), vm((3, TILE_DEV, D_TILE), BF16),
+            vm((4, 3, TILE_DEV, D_TILE), BF16), vm((3, TILE_DEV, D_TILE), BF16), vm((3, TILE_DEV, D_TILE), BF16),
             vm((D_SLIDE, 2 * D_SLIDE), BF16), vm((D_SLIDE, D_SLIDE), BF16), vm((D_SLIDE, D_SLIDE), BF16),
             vm((16, 8, 128), F32), vm((16, 8, 128), F32), vm((8, 8, 128), F32),
             vm((16, 16, 384), BF16), vm((16, 16, 384), BF16), vm((8, 128, D_SLIDE), BF16),
             vm((SEQ, 1024), BF16), vm((SEQ, D_SLIDE), F32), vm((SEQ, D_SLIDE), BF16),
             vm((SEQ, 2 * D_SLIDE), BF16), vm((256, SEQ), F32), vm((SEQ_DEV, D_SLIDE), F32),
-            dma((18,)), dma((4,)), dma((16,)), dma((16,)), dma((4,)), dma((4,)), dma((4,)), dma((4,)),
+            dma((18,)), dma((4,)), dma((16,)), dma((16,)), dma((16,)), dma((16,)), dma((4,)), dma((4,)),
             dma((16,)), dma((16,)), dma((8,)), dma((8,)), dma((16,)), dma((16,)), dma((8,)), dma((8,)),
         ],
         compiler_params=pltpu.CompilerParams(
@@ -389,9 +378,9 @@
         ),
         name="slide_kernel",
     )(
-        tiles, wide(mlp_gain), wide(mlp_bias), gate_weight, up_weight, down_weight, wide(layer_scale),
-        wide(final_gain), wide(final_bias), patch_weight, wide(patch_bias), wide(slide_gain), wide(slide_bias),
-        w_query, w_key, w_value, w_out, slide_lengths, wide(tile_slot),
+        tiles, mlp_gain, mlp_bias, gate_weight, up_weight, down_weight, layer_scale,
+        final_gain, final_bias, patch_weight, patch_bias, slide_gain, slide_bias,
+        w_query, w_key, w_value, w_out, slide_lengths, tile_slot.reshape(1, TILE_DEV),
     )
 
 

time: 78.6 us -> 64.6 us (0.82); the launches traced: 77.2 us -> 64.4 us
  local copies, waits for them, and re-layouts: 11.9 us -> 1.62 us
  Pallas kernels: 65.3 us -> 62.8 us
    reshape x8 -> x0, local copies, waits for them, and re-layouts: 10.3 us -> none  [per_device(): wide = lambda v: v.reshape(1, -1)]
    pallas_call x1, Pallas kernels: 65.3 us -> 62.8 us  [per_device(): pl.pallas_call(kernel, out_shape=jax.ShapeDtypeStruct((1, SEQ_DEV, D_SLID...]
where the time goes in v1:
time: 64.6 us; the launch traced here: 64.4 us
  Pallas kernels  62.8 us (97%)
  local copies, waits for them, and re-layouts  1.62 us (3%)
    pallas_call x1, Pallas kernels, per_device(): pl.pallas_call(kernel, out_shape=jax.ShapeDtypeStruct((1, SEQ_DEV, D_SLID...  62.8 us
    unnamed x1, local copies, waits for them, and re-layouts  1.62 us

profile of v1, /device:TPU:1, one launch (start us, length us, event | category | flops | bytes accessed | tf_op | source)
XLA Modules:
  0.0 64.4 jit_solution(4494964114810435000)
XLA Ops:
  0.0 62.8 %slide_kernel.1 = f32[1,64,768]{2,1,0:T(8,128)} custom-call(f32[32,1536]{1,0:T(8,128)} %tiles_h.1, f32[1536]{0:T(1024)} %mlp_gain_h.1, f32[1536]{0:T(1024)} %mlp_bias_h.1, bf16[1536,256]{1,0:T(8,128)(2,1)} %gate_h.1, bf16[1536,256]{1,0:T(8,128)(2,1)} %up_h.1, bf16[256,1536]{1,0:T(8,128)(2,1)} %down_h.1, f32[1536]{0:T(1024)} %layer_scale_h.1, ...), custom_call_target="tpu_custom_call" | custom-call | tf_op jit(solution)/shard_map/slide_kernel/pallas_call | solution.py:353
  62.8 1.6 %copy.21 = f32[1,64,768]{2,1,0:T(8,128)} copy(f32[1,64,768]{2,1,0:T(8,128)} %slide_kernel.1) | data formatting | bytes 393216

commit v2 on v1

--- a/solution.py
+++ b/solution.py
@@ -58,7 +58,7 @@
         return (s, ((y + (1 - c) * k) % 4) * 4 + (z + c * k) % 4)
 
     def on_tile(k):
-        return (s, (t + k) % 16)
+        return (s, ((y + k // 4) % 4) * 4 + (z + k) % 4)
 
     def on_slide(dx, dc):
         return (((x + dx) % 4) * 2 + (c + dc) % 2, t)
@@ -116,14 +116,40 @@
             rows.at[4 * j], rows.at[4 * j + i], ag2_s.at[4 * j + i], ag_r.at[4 * j + i], second(offset_of(i))
         )
 
-    for i in range(1, 4):
-        ag2(i, 0).start()
-        pending.append(ag2(i, 0).wait_send)
-    for j in range(1, 4):
-        ag1(j).wait_recv()
-        for i in range(1, 4):
+    def side_of(j):
+        return ((j + 1) // 2) % 2
+
+    def pass_on(j):
+        m = side_of(j)
+        return remote(
+            rows.at[4 * j + 1 + m], rows.at[4 * j + 3], ag2_s.at[4 * j + 3], ag_r.at[4 * j + 3], second(1 + 2 * m)
+        )
+
+    def spread(j):
+        for i in range(1, 3):
             ag2(i, j).start()
             pending.append(ag2(i, j).wait_send)
+
+    def relay(j):
+        ag2(1 + side_of(j), j).wait_recv()
+        pass_on(j).start()
+
+    def far_last():
+        return remote(rows.at[12], rows.at[15], ag2_s.at[15], ag_r.at[15], second(2))
+
+    spread(0)
+    for j in range(1, 3):
+        ag1(j).wait_recv()
+        spread(j)
+    relay(0)
+    ag1(3).wait_recv()
+    far_last().start()
+    spread(3)
+    pending.append(far_last().wait_send)
+    relay(1)
+    relay(2)
+    for j in range(3):
+        pending.append(pass_on(j).wait_send)
     for i in range(3, 6):
         loads[i].wait()
 
@@ -133,8 +159,13 @@
         )
 
     def batch(j, carry):
-        for i in range(1, 4):
-            ag2(i, j).wait_recv()
+        ag2(2 - side_of(j), j).wait_recv()
+        pass_on(j).wait_recv()
+
+        @pl.when(j == 3)
+        def _():
+            ag2(1, 3).wait_recv()
+
         block = rows[pl.ds(4 * j, 4)].reshape(128, D_TILE)
         gate_out = jnp.dot(block, gate[...], preferred_element_type=F32)
         up_out = jnp.dot(block, up[...], preferred_element_type=F32)
@@ -142,7 +173,7 @@
         part[pl.ds(4 * j, 4)] = (
             jnp.dot(hidden, down[...], preferred_element_type=F32).astype(BF16).reshape(4, TILE_DEV, D_TILE)
         )
-        for i in range(1, 4):
+        for i in (3, 1, 2):
             rs1(i, j).start()
         return carry
 
@@ -160,7 +191,7 @@
     pos_in[0] = pos_out[t]
 
     def pos_copy(k):
-        return remote(pos_out.at[(t + k) % 16], pos_in.at[k], pos_s.at[k], pos_r.at[k], on_tile(k))
+        return remote(pos_out.at[on_tile(k)[1]], pos_in.at[k], pos_s.at[k], pos_r.at[k], on_tile(k))
 
     def pos_start(k, carry):
         pos_copy(k).start()
@@ -249,7 +280,7 @@
     )
 
     def slot_copy(k):
-        return remote(send_slots.at[(t + k) % 16], got_slots.at[k], sl_s.at[k], sl_r.at[k], on_tile(k))
+        return remote(send_slots.at[on_tile(k)[1]], got_slots.at[k], sl_s.at[k], sl_r.at[k], on_tile(k))
 
     def slot_start(k, carry):
         slot_copy(k).start()
@@ -268,44 +299,64 @@
     for k in range(8):
         one_hot[:, k * 128 : (k + 1) * 128] = jnp.where(position == pos_all[k][0:1], 1.0, 0.0).astype(BF16)
 
-    def slot_wait(k, carry):
-        slot_copy(k).wait_recv()
-        return carry
-
-    lax.fori_loop(1, 16, slot_wait, 0)
-    wide = got_slots[...].astype(F32)
-    slots[0, :, 0:384] = wide[:, 0:8, :].reshape(128, 384).astype(BF16)
-    slots[0, :, 384:768] = wide[:, 8:16, :].reshape(128, 384).astype(BF16)
-
-    def far(i):
-        k = 2 * offset_of(i)
-        return remote(slots.at[0], slots.at[k], dg_s.at[k], dg_r.at[k], on_slide(offset_of(i), 0))
-
-    def near(i):
-        k = 2 * offset_of(i)
-        return remote(slots.at[k], slots.at[k + 1], dg_s.at[k + 1], dg_r.at[k + 1], on_slide(0, 1))
-
-    for i in range(1, 4):
-        far(i).start()
-        pending.append(far(i).wait_send)
-    near(0).start()
-    pending.append(near(0).wait_send)
-
-    def place_pair(i):
-        k = 2 * offset_of(i)
+    def along(e, q, dx):
+        return remote(slots.at[0, q], slots.at[e, q], dg_s.at[4 * e + q], dg_r.at[4 * e + q], on_slide(dx, 0))
+
+    def far_on(q):
+        return remote(
+            slots.at[2 + 4 * c, q], slots.at[4, q], dg_s.at[16 + q], dg_r.at[16 + q], on_slide(1 + 2 * c, 0)
+        )
+
+    def near(e, q):
+        at = 4 * e + 4 + q
+        return remote(slots.at[e, q], slots.at[e + 1, q], dg_s.at[at], dg_r.at[at], on_slide(0, 1))
+
+    order = (0, 1, 3, 2)
+    for q in order:
+        for k in range(4 * q, 4 * q + 4):
+            if k > 0:
+                slot_copy(k).wait_recv()
+        wide = got_slots[4 * q : 4 * q + 4].astype(F32)
+        slots[0, q, :, 0:384] = wide[:, 0:8, :].reshape(32, 384).astype(BF16)
+        slots[0, q, :, 384:768] = wide[:, 8:16, :].reshape(32, 384).astype(BF16)
+        if q == order[3]:
+            along(4, q, 2).start()
+            pending.append(along(4, q, 2).wait_send)
+        along(2, q, 1).start()
+        along(6, q, 3).start()
+        near(0, q).start()
+        pending.append(along(2, q, 1).wait_send)
+        pending.append(along(6, q, 3).wait_send)
+        pending.append(near(0, q).wait_send)
+
+    def came(e, q):
+        along(e, q, 0).wait_recv()
+        near(e, q).start()
+        pending.append(near(e, q).wait_send)
+
+    for q in order:
+        along(2 + 4 * c, q, 0).wait_recv()
+        if q != order[3]:
+            far_on(q).start()
+            pending.append(far_on(q).wait_send)
+        near(2 + 4 * c, q).start()
+        pending.append(near(2 + 4 * c, q).wait_send)
+        came(6 - 4 * c, q)
+
+    def place_pair(k):
         return jnp.dot(
             one_hot[:, k * 128 : (k + 2) * 128], slots[k : k + 2].reshape(256, D_SLIDE), preferred_element_type=F32
         )
 
-    near(0).wait_recv()
+    for q in order:
+        near(0, q).wait_recv()
     canvas[...] = place_pair(0)
-    for i in range(1, 4):
-        far(i).wait_recv()
-        near(i).start()
-        pending.append(near(i).wait_send)
-    for i in range(1, 4):
-        near(i).wait_recv()
-        canvas[...] += place_pair(i)
+    for q in order:
+        came(4, q)
+    for k in (2, 6, 4):
+        for q in order:
+            near(k, q).wait_recv()
+        canvas[...] += place_pair(k)
     for i in range(16, 18):
         loads[i].wait()
     normed_all[...] = layer_norm(canvas[...], slide_gain[...], slide_bias[...]).astype(BF16)
@@ -367,11 +418,11 @@
             vm((4, 3, TILE_DEV, D_TILE), BF16), vm((3, TILE_DEV, D_TILE), BF16), vm((3, TILE_DEV, D_TILE), BF16),
             vm((D_SLIDE, 2 * D_SLIDE), BF16), vm((D_SLIDE, D_SLIDE), BF16), vm((D_SLIDE, D_SLIDE), BF16),
             vm((16, 8, 128), F32), vm((16, 8, 128), F32), vm((8, 8, 128), F32),
-            vm((16, 16, 384), BF16), vm((16, 16, 384), BF16), vm((8, 128, D_SLIDE), BF16),
+            vm((16, 16, 384), BF16), vm((16, 16, 384), BF16), vm((8, 4, 32, D_SLIDE), BF16),
             vm((SEQ, 1024), BF16), vm((SEQ, D_SLIDE), F32), vm((SEQ, D_SLIDE), BF16),
             vm((SEQ, 2 * D_SLIDE), BF16), vm((256, SEQ), F32), vm((SEQ_DEV, D_SLIDE), F32),
             dma((18,)), dma((4,)), dma((16,)), dma((16,)), dma((16,)), dma((16,)), dma((4,)), dma((4,)),
-            dma((16,)), dma((16,)), dma((8,)), dma((8,)), dma((16,)), dma((16,)), dma((8,)), dma((8,)),
+            dma((16,)), dma((16,)), dma((8,)), dma((8,)), dma((16,)), dma((16,)), dma((32,)), dma((32,)),
         ],
         compiler_params=pltpu.CompilerParams(
             collective_id=0, has_side_effects=True, vmem_limit_bytes=56 * 2**20

time: 64.6 us -> 63.6 us (0.985)
  Pallas kernels: 62.8 us -> 61.8 us
    pallas_call x1, Pallas kernels: 62.8 us -> 61.8 us  [per_device(): pl.pallas_call(kernel, out_shape=jax.ShapeDtypeStruct((1, SEQ_DEV, D_SLID...]
where the time goes in v2:
time: 63.6 us; the launch traced here: 63.5 us
  Pallas kernels  61.8 us (97%)
  local copies, waits for them, and re-layouts  1.62 us (3%)
    pallas_call x1, Pallas kernels, per_device(): pl.pallas_call(kernel, out_shape=jax.ShapeDtypeStruct((1, SEQ_DEV, D_SLID...  61.8 us
    unnamed x1, local copies, waits for them, and re-layouts  1.62 us

profile of v2, /device:TPU:1, one launch (start us, length us, event | category | flops | bytes accessed | tf_op | source)
XLA Modules:
  0.0 63.5 jit_solution(17116912373659929612)
XLA Ops:
  0.0 61.8 %slide_kernel.1 = f32[1,64,768]{2,1,0:T(8,128)} custom-call(f32[32,1536]{1,0:T(8,128)} %tiles_h.1, f32[1536]{0:T(1024)} %mlp_gain_h.1, f32[1536]{0:T(1024)} %mlp_bias_h.1, bf16[1536,256]{1,0:T(8,128)(2,1)} %gate_h.1, bf16[1536,256]{1,0:T(8,128)(2,1)} %up_h.1, bf16[256,1536]{1,0:T(8,128)(2,1)} %down_h.1, f32[1536]{0:T(1024)} %layer_scale_h.1, ...), custom_call_target="tpu_custom_call" | custom-call | tf_op jit(solution)/shard_map/slide_kernel/pallas_call | solution.py:404
  61.9 1.6 %copy.21 = f32[1,64,768]{2,1,0:T(8,128)} copy(f32[1,64,768]{2,1,0:T(8,128)} %slide_kernel.1) | data formatting | bytes 393216

commit v3 on v2

--- a/solution.py
+++ b/solution.py
@@ -116,40 +116,29 @@
             rows.at[4 * j], rows.at[4 * j + i], ag2_s.at[4 * j + i], ag_r.at[4 * j + i], second(offset_of(i))
         )
 
-    def side_of(j):
-        return ((j + 1) // 2) % 2
-
-    def pass_on(j):
-        m = side_of(j)
-        return remote(
-            rows.at[4 * j + 1 + m], rows.at[4 * j + 3], ag2_s.at[4 * j + 3], ag_r.at[4 * j + 3], second(1 + 2 * m)
-        )
-
     def spread(j):
         for i in range(1, 3):
             ag2(i, j).start()
             pending.append(ag2(i, j).wait_send)
 
-    def relay(j):
-        ag2(1 + side_of(j), j).wait_recv()
-        pass_on(j).start()
-
-    def far_last():
-        return remote(rows.at[12], rows.at[15], ag2_s.at[15], ag_r.at[15], second(2))
+    def far_chunk(j):
+        return remote(rows.at[4 * j], rows.at[4 * j + 3], ag2_s.at[4 * j + 3], ag_r.at[4 * j + 3], second(2))
 
     spread(0)
-    for j in range(1, 3):
-        ag1(j).wait_recv()
-        spread(j)
-    relay(0)
+    far_chunk(0).start()
+    ag1(1).wait_recv()
+    spread(1)
+    far_chunk(1).start()
+    ag1(2).wait_recv()
+    spread(2)
+    far_chunk(2).start()
     ag1(3).wait_recv()
-    far_last().start()
+    far_chunk(3).start()
     spread(3)
-    pending.append(far_last().wait_send)
-    relay(1)
-    relay(2)
-    for j in range(3):
-        pending.append(pass_on(j).wait_send)
+    pending.append(far_chunk(0).wait_send)
+    pending.append(far_chunk(1).wait_send)
+    pending.append(far_chunk(2).wait_send)
+    pending.append(far_chunk(3).wait_send)
     for i in range(3, 6):
         loads[i].wait()
 
@@ -159,12 +148,9 @@
         )
 
     def batch(j, carry):
-        ag2(2 - side_of(j), j).wait_recv()
-        pass_on(j).wait_recv()
-
-        @pl.when(j == 3)
-        def _():
-            ag2(1, 3).wait_recv()
+        ag2(1, j).wait_recv()
+        ag2(2, j).wait_recv()
+        far_chunk(j).wait_recv()
 
         block = rows[pl.ds(4 * j, 4)].reshape(128, D_TILE)
         gate_out = jnp.dot(block, gate[...], preferred_element_type=F32)
@@ -302,11 +288,6 @@
     def along(e, q, dx):
         return remote(slots.at[0, q], slots.at[e, q], dg_s.at[4 * e + q], dg_r.at[4 * e + q], on_slide(dx, 0))
 
-    def far_on(q):
-        return remote(
-            slots.at[2 + 4 * c, q], slots.at[4, q], dg_s.at[16 + q], dg_r.at[16 + q], on_slide(1 + 2 * c, 0)
-        )
-
     def near(e, q):
         at = 4 * e + 4 + q
         return remote(slots.at[e, q], slots.at[e + 1, q], dg_s.at[at], dg_r.at[at], on_slide(0, 1))
@@ -319,9 +300,8 @@
         wide = got_slots[4 * q : 4 * q + 4].astype(F32)
         slots[0, q, :, 0:384] = wide[:, 0:8, :].reshape(32, 384).astype(BF16)
         slots[0, q, :, 384:768] = wide[:, 8:16, :].reshape(32, 384).astype(BF16)
-        if q == order[3]:
-            along(4, q, 2).start()
-            pending.append(along(4, q, 2).wait_send)
+        along(4, q, 2).start()
+        pending.append(along(4, q, 2).wait_send)
         along(2, q, 1).start()
         along(6, q, 3).start()
         near(0, q).start()
@@ -336,9 +316,6 @@
 
     for q in order:
         along(2 + 4 * c, q, 0).wait_recv()
-        if q != order[3]:
-            far_on(q).start()
-            pending.append(far_on(q).wait_send)
         near(2 + 4 * c, q).start()
         pending.append(near(2 + 4 * c, q).wait_send)
         came(6 - 4 * c, q)
@@ -403,7 +380,7 @@
     vm = pltpu.VMEM
     return pl.pallas_call(
         kernel,
-        out_shape=jax.ShapeDtypeStruct((1, SEQ_DEV, D_SLIDE), F32),
+        out_shape=pltpu.VMEM((1, SEQ_DEV, D_SLIDE), F32),
         in_specs=[hbm] * 17 + [pl.BlockSpec(memory_space=pltpu.SMEM)] + [hbm],
         out_specs=pl.BlockSpec(memory_space=pltpu.VMEM),
         scratch_shapes=[

time: 63.6 us -> 60.7 us (0.954)
  Pallas kernels: 61.8 us -> 59.9 us
  local copies, waits for them, and re-layouts: 1.62 us -> 0.68 us
    pallas_call x1, Pallas kernels: 61.8 us -> 59.9 us  [per_device(): pl.pallas_call(kernel, out_shape=pltpu.VMEM((1, SEQ_DEV, D_SLIDE), F32),...]
    unnamed x1, local copies, waits for them, and re-layouts: 1.62 us -> 0.68 us
where the time goes in v3:
time: 60.7 us; the launch traced here: 60.5 us
  Pallas kernels  59.9 us (99%)
  local copies, waits for them, and re-layouts  0.68 us (1%)
    pallas_call x1, Pallas kernels, per_device(): pl.pallas_call(kernel, out_shape=pltpu.VMEM((1, SEQ_DEV, D_SLIDE), F32),...  59.9 us

profile of v3, /device:TPU:1, one launch (start us, length us, event | category | flops | bytes accessed | tf_op | source)
XLA Modules:
  0.0 60.5 jit_solution(7854577293408500139)
XLA Ops:
  0.0 59.9 %slide_kernel.1 = f32[1,64,768]{2,1,0:T(8,128)S(1)} custom-call(f32[32,1536]{1,0:T(8,128)} %tiles_h.1, f32[1536]{0:T(1024)} %mlp_gain_h.1, f32[1536]{0:T(1024)} %mlp_bias_h.1, bf16[1536,256]{1,0:T(8,128)(2,1)} %gate_h.1, bf16[1536,256]{1,0:T(8,128)(2,1)} %up_h.1, bf16[256,1536]{1,0:T(8,128)(2,1)} %down_h.1, f32[1536]{0:T(1024)} %layer_scale_h.1, ...), custom_call_target="tpu_custom_call" | custom-call | tf_op jit(solution)/shard_map/slide_kernel/pallas_call | solution.py:381
  59.9 0.7 %copy.21 = f32[1,64,768]{2,1,0:T(8,128)} copy(f32[1,64,768]{2,1,0:T(8,128)S(1)} %slide_kernel.1) | data formatting | bytes 393216

commit v4 on v3

--- a/solution.py
+++ b/solution.py
@@ -37,10 +37,10 @@
 
 def kernel(
     tiles_h, mlp_gain_h, mlp_bias_h, gate_h, up_h, down_h, layer_scale_h, final_gain_h, final_bias_h,
-    patch_h, patch_bias_h, slide_gain_h, slide_bias_h, wq_h, wk_h, wv_h, wo_h, lengths, slot_h,
+    patch_h, patch_bias_h, slide_gain_h, slide_bias_h, wq_h, wk_h, wv_h, wo_h, lengths_h, slot_h,
     out,
     tiles, mlp_gain, mlp_bias, gate, up, down, layer_scale, final_gain, final_bias,
-    patch, patch_bias, slide_gain, slide_bias, wq, wk, wv, wo, slot,
+    patch, patch_bias, slide_gain, slide_bias, wq, wk, wv, wo, slot, lengths,
     rows, part, got1, fold, got2, wkv16, wq16, wo16,
     pos_out, pos_in, pos_all, send_slots, got_slots, slots, one_hot, canvas, normed_all, kv, mult, att,
     load_sem, ag1_s, ag2_s, ag_r, rs1_s, rs1_r, rs2_s, rs2_r,
@@ -71,6 +71,11 @@
 
     pending = []
 
+    def drain():
+        for wait in pending:
+            wait()
+        pending.clear()
+
     def sent(copy, first_k, last_k):
         def one(k, carry):
             copy(k).wait_send()
@@ -83,20 +88,25 @@
     def greet(device):
         pl.semaphore_signal(barrier, inc=1, device_id=device, device_id_type=MESH)
 
-    for k in range(1, 4):
-        greet(first(k))
-        greet(second(k))
-    for k in range(1, 8):
-        greet(on_slide(k // 2, k % 2))
+    def greetings():
+        for k in range(1, 4):
+            greet(first(k))
+            greet(second(k))
+        for k in range(1, 8):
+            greet(on_slide(k // 2, k % 2))
 
     pairs = (
         (tiles_h, tiles), (mlp_gain_h, mlp_gain), (mlp_bias_h, mlp_bias),
         (gate_h, gate), (up_h, up), (down_h, down), (slot_h, slot), (layer_scale_h, layer_scale),
         (final_gain_h, final_gain), (final_bias_h, final_bias), (patch_h, patch), (patch_bias_h, patch_bias),
         (wk_h, wk), (wv_h, wv), (wq_h, wq), (wo_h, wo), (slide_gain_h, slide_gain), (slide_bias_h, slide_bias),
+        (lengths_h, lengths),
     )
     loads = [pltpu.make_async_copy(a, b, load_sem.at[i]) for i, (a, b) in enumerate(pairs)]
-    for load in loads:
+    for load in loads[:3]:
+        load.start()
+    greetings()
+    for load in loads[3:]:
         load.start()
     for i in range(3):
         loads[i].wait()
@@ -123,6 +133,18 @@
 
     def far_chunk(j):
         return remote(rows.at[4 * j], rows.at[4 * j + 3], ag2_s.at[4 * j + 3], ag_r.at[4 * j + 3], second(2))
+
+    loads[18].wait()
+    length = lengths[t]
+    row = iota((256, SEQ), 0)
+    key = iota((256, SEQ), 1)
+    head, query = row // 64, row % 64
+    weight = (
+        1.0
+        + jnp.where((query % 2 == head % 2) & (key % 2 == head % 2), 1.0, 0.0)
+        + jnp.where((query % 4 == head) & (key % 4 == head), 1.0, 0.0)
+    )
+    mult[...] = jnp.where(key < length, weight, 0.0)
 
     spread(0)
     far_chunk(0).start()
@@ -199,17 +221,6 @@
 
     lax.fori_loop(0, 6, convert, 0)
 
-    length = lengths[t]
-    row = iota((256, SEQ), 0)
-    key = iota((256, SEQ), 1)
-    head, query = row // 64, row % 64
-    weight = (
-        1.0
-        + jnp.where((query % 2 == head % 2) & (key % 2 == head % 2), 1.0, 0.0)
-        + jnp.where((query % 4 == head) & (key % 4 == head), 1.0, 0.0)
-    )
-    mult[...] = jnp.where(key < length, weight, 0.0)
-
     def rs2(j):
         return remote(fold.at[j - 1], got2.at[j - 1], rs2_s.at[j], rs2_r.at[j], first(4 - offset_of(j)))
 
@@ -273,6 +284,7 @@
         return carry
 
     lax.fori_loop(1, 16, slot_start, 0)
+    drain()
     sent(slot_copy, 1, 16)
     got_slots[0] = send_slots[t]
 
@@ -314,22 +326,22 @@
         near(e, q).start()
         pending.append(near(e, q).wait_send)
 
-    for q in order:
-        along(2 + 4 * c, q, 0).wait_recv()
-        near(2 + 4 * c, q).start()
-        pending.append(near(2 + 4 * c, q).wait_send)
-        came(6 - 4 * c, q)
-
     def place_pair(k):
         return jnp.dot(
             one_hot[:, k * 128 : (k + 2) * 128], slots[k : k + 2].reshape(256, D_SLIDE), preferred_element_type=F32
         )
 
+    def arrive(q):
+        for e in (2 + 4 * c, 6 - 4 * c, 4):
+            came(e, q)
+
+    drain()
+    for q in order[:3]:
+        arrive(q)
     for q in order:
         near(0, q).wait_recv()
     canvas[...] = place_pair(0)
-    for q in order:
-        came(4, q)
+    arrive(order[3])
     for k in (2, 6, 4):
         for q in order:
             near(k, q).wait_recv()
@@ -367,8 +379,7 @@
     here = iota((SEQ_DEV, D_SLIDE), 0) + s * SEQ_DEV
     out[0] = jnp.where(here < length, result, 0.0)
 
-    for wait in pending:
-        wait()
+    drain()
 
 
 def per_device(
@@ -381,7 +392,7 @@
     return pl.pallas_call(
         kernel,
         out_shape=pltpu.VMEM((1, SEQ_DEV, D_SLIDE), F32),
-        in_specs=[hbm] * 17 + [pl.BlockSpec(memory_space=pltpu.SMEM)] + [hbm],
+        in_specs=[hbm] * 19,
         out_specs=pl.BlockSpec(memory_space=pltpu.VMEM),
         scratch_shapes=[
             vm((TILE_DEV, D_TILE), F32), vm((D_TILE,), F32), vm((D_TILE,), F32),
@@ -390,7 +401,7 @@
             vm((D_TILE, D_SLIDE), BF16), vm((D_SLIDE,), F32), vm((D_SLIDE,), F32), vm((D_SLIDE,), F32),
             vm((D_SLIDE, D_SLIDE), F32), vm((D_SLIDE, D_SLIDE), F32),
             vm((D_SLIDE, D_SLIDE), F32), vm((D_SLIDE, D_SLIDE), F32),
-            vm((1, TILE_DEV), jnp.int32),
+            vm((1, TILE_DEV), jnp.int32), pltpu.SMEM((16,), jnp.int32),
             vm((16, TILE_DEV, D_TILE), BF16), vm((16, TILE_DEV, D_TILE), BF16),
             vm((4, 3, TILE_DEV, D_TILE), BF16), vm((3, TILE_DEV, D_TILE), BF16), vm((3, TILE_DEV, D_TILE), BF16),
             vm((D_SLIDE, 2 * D_SLIDE), BF16), vm((D_SLIDE, D_SLIDE), BF16), vm((D_SLIDE, D_SLIDE), BF16),
@@ -398,7 +409,7 @@
             vm((16, 16, 384), BF16), vm((16, 16, 384), BF16), vm((8, 4, 32, D_SLIDE), BF16),
             vm((SEQ, 1024), BF16), vm((SEQ, D_SLIDE), F32), vm((SEQ, D_SLIDE), BF16),
             vm((SEQ, 2 * D_SLIDE), BF16), vm((256, SEQ), F32), vm((SEQ_DEV, D_SLIDE), F32),
-            dma((18,)), dma((4,)), dma((16,)), dma((16,)), dma((16,)), dma((16,)), dma((4,)), dma((4,)),
+            dma((19,)), dma((4,)), dma((16,)), dma((16,)), dma((16,)), dma((16,)), dma((4,)), dma((4,)),
             dma((16,)), dma((16,)), dma((8,)), dma((8,)), dma((16,)), dma((16,)), dma((32,)), dma((32,)),
         ],
         compiler_params=pltpu.CompilerParams(

time: 60.7 us -> 59.9 us (0.987)
  Pallas kernels: 59.9 us -> 59.1 us
    pallas_call x1, Pallas kernels: 59.9 us -> 59.1 us  [per_device(): pl.pallas_call(kernel, out_shape=pltpu.VMEM((1, SEQ_DEV, D_SLIDE), F32),...]
where the time goes in v4:
time: 59.9 us; the launch traced here: 59.8 us
  Pallas kernels  59.1 us (99%)
  local copies, waits for them, and re-layouts  0.68 us (1%)
    pallas_call x1, Pallas kernels, per_device(): pl.pallas_call(kernel, out_shape=pltpu.VMEM((1, SEQ_DEV, D_SLIDE), F32),...  59.1 us

profile of v4, /device:TPU:1, one launch (start us, length us, event | category | flops | bytes accessed | tf_op | source)
XLA Modules:
  0.0 59.8 jit_solution(5171843430379057658)
XLA Ops:
  0.0 59.1 %slide_kernel.1 = f32[1,64,768]{2,1,0:T(8,128)S(1)} custom-call(f32[32,1536]{1,0:T(8,128)} %tiles_h.1, f32[1536]{0:T(1024)} %mlp_gain_h.1, f32[1536]{0:T(1024)} %mlp_bias_h.1, bf16[1536,256]{1,0:T(8,128)(2,1)} %gate_h.1, bf16[1536,256]{1,0:T(8,128)(2,1)} %up_h.1, bf16[256,1536]{1,0:T(8,128)(2,1)} %down_h.1, f32[1536]{0:T(1024)} %layer_scale_h.1, ...), custom_call_target="tpu_custom_call" | custom-call | tf_op jit(solution)/shard_map/slide_kernel/pallas_call | solution.py:392
  59.1 0.7 %copy.21 = f32[1,64,768]{2,1,0:T(8,128)} copy(f32[1,64,768]{2,1,0:T(8,128)S(1)} %slide_kernel.1) | data formatting | bytes 393216

commit v5 on v4

--- a/solution.py
+++ b/solution.py
@@ -304,6 +304,10 @@
         at = 4 * e + 4 + q
         return remote(slots.at[e, q], slots.at[e + 1, q], dg_s.at[at], dg_r.at[at], on_slide(0, 1))
 
+    def across(e, q, dx):
+        at = 4 * e + 4 + q
+        return remote(slots.at[0, q], slots.at[e + 1, q], dg_s.at[at], dg_r.at[at], on_slide(dx, 1))
+
     order = (0, 1, 3, 2)
     for q in order:
         for k in range(4 * q, 4 * q + 4):
@@ -317,14 +321,19 @@
         along(2, q, 1).start()
         along(6, q, 3).start()
         near(0, q).start()
+        if q == order[3]:
+            for e, dx in ((4, 2), (2, 1), (6, 3)):
+                across(e, q, dx).start()
+                pending.append(across(e, q, dx).wait_send)
         pending.append(along(2, q, 1).wait_send)
         pending.append(along(6, q, 3).wait_send)
         pending.append(near(0, q).wait_send)
 
     def came(e, q):
         along(e, q, 0).wait_recv()
-        near(e, q).start()
-        pending.append(near(e, q).wait_send)
+        if q != order[3]:
+            near(e, q).start()
+            pending.append(near(e, q).wait_send)
 
     def place_pair(k):
         return jnp.dot(

time: 59.9 us -> 59.9 us (level)
  no operation moved by 1% of the time
where the time goes in v5:
time: 59.9 us; the launch traced here: 59.8 us
  Pallas kernels  59.2 us (99%)
  local copies, waits for them, and re-layouts  0.68 us (1%)
    pallas_call x1, Pallas kernels, per_device(): pl.pallas_call(kernel, out_shape=pltpu.VMEM((1, SEQ_DEV, D_SLIDE), F32),...  59.2 us

profile of v5, /device:TPU:1, one launch (start us, length us, event | category | flops | bytes accessed | tf_op | source)
XLA Modules:
  0.0 59.8 jit_solution(2295724214891099930)
XLA Ops:
  0.0 59.2 %slide_kernel.1 = f32[1,64,768]{2,1,0:T(8,128)S(1)} custom-call(f32[32,1536]{1,0:T(8,128)} %tiles_h.1, f32[1536]{0:T(1024)} %mlp_gain_h.1, f32[1536]{0:T(1024)} %mlp_bias_h.1, bf16[1536,256]{1,0:T(8,128)(2,1)} %gate_h.1, bf16[1536,256]{1,0:T(8,128)(2,1)} %up_h.1, bf16[256,1536]{1,0:T(8,128)(2,1)} %down_h.1, f32[1536]{0:T(1024)} %layer_scale_h.1, ...), custom_call_target="tpu_custom_call" | custom-call | tf_op jit(solution)/shard_map/slide_kernel/pallas_call | solution.py:401
  59.2 0.7 %copy.21 = f32[1,64,768]{2,1,0:T(8,128)} copy(f32[1,64,768]{2,1,0:T(8,128)S(1)} %slide_kernel.1) | data formatting | bytes 393216
